TPU v7x, 256 devices: a whole 4x4x8 slice. The times are simulated.
256 devices in a mesh: pair: 64 (over y, z, core), virt: 4 (over x).
Axes of the slice: x: 4, y: 4, z: 8, core: 2. Of those that a mesh axis runs over, the one named last changes fastest.
Arguments:
- amplitudes: bfloat16 [256, 512, 512], P('pair', 'virt'), may hold values from -6 to 6
- panels: bfloat16 [16, 512, 512], P('virt', 'pair'), may hold values from -0.125 to 0.125
- domain: int32 [256, 8, 8], P('pair'), may hold values 0 or 1
- mirror: int32 [256], P('pair'), may hold values from 0 to 255, as said below
Outputs:
- symmetrized: float32 [256, 512, 512], P('pair', None, 'virt')
Inputs may be any that keep to these rules, and one draw needn't show every extreme that they name: mirror is an involution without fixed points; a pair of group g (pairs g * 4 to g * 4 + 3) has its mirror in group g XOR (32), and the pairs of each such couple of groups correspond one to one.
All inputs are finite; a program needn't handle non-finite values. No bound on the sum of `domain` on one device may be relied on, other than what follows from the above.
Results may differ from a plain program's by a relative error of at most 0.0029.
Values may be sent and summed in bfloat16 or wider, within the bound.
A program may use at most 64 MiB of HBM per device.

v0:
```python
import jax
import jax.numpy as jnp
from jax import lax
from jax.sharding import PartitionSpec as P


def partner_2(block, axis, bit):
    count = lax.axis_size(axis)
    route = []
    for low in range(count):
        high = low | 1 << bit
        if high != low and high < count:
            route += [(low, high), (high, low)]
    return lax.ppermute(block, axis, route)


def expand_mask(domain_tiles, tile_size):
    pair_count = domain_tiles.shape[0]
    tile_count = domain_tiles.shape[1]
    spread = jnp.broadcast_to(
        domain_tiles[:, :, None, :, None],
        (pair_count, tile_count, tile_size, tile_count, tile_size),
    )
    return spread.reshape(pair_count, tile_count * tile_size, tile_count * tile_size)


def body(amplitudes, panels, domain, mirror):
    pair_count = amplitudes.shape[0]
    row_share = amplitudes.shape[1]
    full_width = amplitudes.shape[2]
    tile_size = full_width // domain.shape[1]
    offset = lax.axis_index("virt") * row_share
    blocks = lax.all_gather(panels, "virt", axis=0, tiled=True)
    panels_all = lax.all_gather(blocks, "pair", axis=1, tiled=True)
    mask_full = expand_mask(domain, tile_size).astype(jnp.bfloat16)
    mask_rows = lax.dynamic_slice_in_dim(mask_full, offset, row_share, 1)
    masked = amplitudes * mask_rows
    half_done = jnp.einsum(
        "pcd,qbd->qpcb", masked, panels_all, preferred_element_type=jnp.float32
    ).astype(jnp.bfloat16)
    panel_cols = lax.dynamic_slice_in_dim(panels_all, offset, row_share, 2)
    own_rows = lax.psum_scatter(
        jnp.einsum("qac,qpcb->apb", panel_cols, half_done, preferred_element_type=jnp.float32),
        "virt",
        scatter_dimension=0,
        tiled=True,
    )
    own_cols = lax.all_to_all(own_rows, "virt", split_axis=2, concat_axis=0, tiled=True)
    swap_bit = lax.axis_size("pair").bit_length() - 2
    partner = partner_2(own_rows, "pair", swap_bit)
    picked = jnp.take(partner, mirror % pair_count, axis=1)
    mask_cols = lax.dynamic_slice_in_dim(mask_full, offset, row_share, 2).astype(jnp.float32)
    return mask_cols * (jnp.transpose(own_cols, (1, 0, 2)) + jnp.transpose(picked, (1, 2, 0)))


def solution(mesh):
    in_specs = (P("pair", "virt", None), P("virt", "pair", None), P("pair", None, None), P("pair"))
    out_specs = P("pair", None, "virt")
    return jax.shard_map(body, mesh=mesh, in_specs=in_specs, out_specs=out_specs, check_vma=False)
```

profile of v0, /device:TPU:24, one launch (start us, length us, event | category | flops | bytes accessed | tf_op | source)
XLA Modules:
  0.0 207.4 jit_solution(1079102553816940406)
XLA Ops:
  6.5 0.0 all-gather.2.cloned.1.call-start
  6.5 13.8 %all_gather.6 = bf16[16,8,512]{2,1,0:T(8,128)(2,1)} all-gather(bf16[4,8,512]{2,1,0:T(8,128)(2,1)} %param.5), channel_id=1, replica_groups=mesh['pair'=64,'virt'=4] {'virt'}, dimensions={0}, use_global_device_ids=true | all-gather | bytes 163840 | tf_op jit(solution)/shard_map/all_gather | solution.py:33
  20.4 0.0 all-gather.2.cloned.1.call-update
  20.4 0.0 reduce-scatter.2.cloned.1.call-start
  20.4 0.7 convert_element_type.16
  21.2 0.1 copy.9
  21.3 2.6 %broadcast_in_dim.18 = bf16[4,8,64,8,64]{2,1,4,3,0:T(8,128)(2,1)} broadcast(bf16[4,8,8]{1,2,0:T(8,128)(2,1)S(1)} %copy.9), dimensions={0,1,3} | broadcast | bytes 2097664 | tf_op jit(solution)/shard_map/broadcast_in_dim | solution.py:20
  23.8 0.0 copy-start.1
  23.8 5.4 %convert_element_type.17 = bf16[4,512,512]{1,2,0:T(8,128)(2,1)S(1)} reshape(bf16[4,8,64,8,64]{2,1,4,3,0:T(8,128)(2,1)} %broadcast_in_dim.18) | data formatting | bytes 4194304 | tf_op jit(solution)/shard_map/convert_element_type | solution.py:35
  29.3 0.0 copy-done.1
  29.3 0.0 copy-start
  29.3 0.3 copy.10
  29.6 78.5 %all-gather.2.cloned.1.call-done = bf16[16,512,512]{2,1,0:T(8,128)(2,1)} async-done(((bf16[16,8,512]{2,1,0:T(8,128)(2,1)}), bf16[16,512,512]{2,1,0:T(8,128)(2,1)}) %all-gather.2.cloned.1.call-update) | async-done | bytes 8388624 | tf_op jit(solution)/shard_map/all_gather | solution.py:34
  108.1 13.4 %fusion.5 = f32[512,4,512]{2,0,1:T(8,128)} fusion(bf16[16,512,512]{2,1,0:T(8,128)(2,1)} %all-gather.2.cloned.1.call-done, s32[]{:T(128)S(6)} %select_n.25, bf16[4,128,512]{1,2,0:T(8,128)(2,1)S(1)} %copy.10, bf16[4,512,512]{1,2,0:T(8,128)(2,1)S(1)} %convert_element_type.17), kind=kOutput, calls=%fused_computation.6 | convolution fusion | flops 8595177472 | bytes 15729664 | tf_op jit(solution)/shard_map/qac,qpcb->apb/dot_general | solution.py:43
  121.5 0.0 copy-done
  121.5 0.0 copy-start.2
  121.5 0.0 reduce-scatter.2.cloned.1.call-update
  121.5 49.1 %reduce-scatter.2.cloned.1.call-done = f32[128,4,512]{2,0,1:T(8,128)} async-done(((f32[512,4,512]{2,0,1:T(8,128)}), f32[128,4,512]{2,0,1:T(8,128)}) %reduce-scatter.2.cloned.1.call-update) | async-done | bytes 1048592 | tf_op jit(solution)/shard_map/reduce_scatter | solution.py:42
  170.6 1.4 collective-permute-start
  172.0 2.6 %copy.11 = f32[128,4,512]{0,1,2:T(4,128)} copy(f32[128,4,512]{2,0,1:T(8,128)} %reduce-scatter.2.cloned.1.call-done) | data formatting | bytes 2097152 | tf_op jit(solution)/shard_map/reduce_scatter | solution.py:42
  174.6 3.5 %all-to-all-start = ((f32[128,4,512]{0,1,2:T(4,128)}), f32[128,4,512]{0,1,2:T(4,128)S(1)}, u32[]{:S(2)}, u32[]{:S(2)}) async-start(f32[128,4,512]{0,1,2:T(4,128)} %copy.11), calls=%async_computation.1 | async-start | bytes 2097152 | tf_op jit(solution)/shard_map/all_to_all | solution.py:48
  178.1 0.0 copy-done.2
  178.1 15.1 %all-to-all-done = f32[128,4,512]{0,1,2:T(4,128)S(1)} async-done(((f32[128,4,512]{0,1,2:T(4,128)}), f32[128,4,512]{0,1,2:T(4,128)S(1)}, u32[]{:S(2)}, u32[]{:S(2)}) %all-to-all-start) | async-done | bytes 1048608 | tf_op jit(solution)/shard_map/all_to_all | solution.py:48
  193.2 0.7 copy.17
  193.9 0.4 all_to_all.16
  194.3 2.9 %collective-permute-done = f32[128,4,512]{2,0,1:T(8,128)S(1)} collective-permute-done((f32[128,4,512]{2,0,1:T(8,128)}, f32[128,4,512]{2,0,1:T(8,128)S(1)}, u32[]{:S(2)}, u32[]{:S(2)}) %collective-permute-start) | collective-permute-done | bytes 1048608 | tf_op jit(solution)/shard_map/ppermute | solution.py:14
  197.3 0.6 gather_fusion
  197.9 1.4 fusion.14
  199.3 1.3 copy.13
  (2 shorter events, 0.0 us)
Async XLA Ops:
  6.5 101.5 %all-gather.2.cloned.1.call-start = ((), (), s32[]{:S(2)}) async-start(), calls=%async_computation.2 | async-start | bytes 8519680 | tf_op jit(solution)/shard_map/all_gather | solution.py:34
  20.4 150.2 %reduce-scatter.2.cloned.1.call-start = ((), (), s32[]{:S(2)}) async-start(), calls=%async_computation.3 | async-start | bytes 5242880 | tf_op jit(solution)/shard_map/reduce_scatter | solution.py:42
  23.8 5.5 %copy-start.1 = (bf16[4,128,512]{2,1,0:T(8,128)(2,1)S(1)}, bf16[4,128,512]{2,1,0:T(8,128)(2,1)}, u32[]{:S(2)}) copy-start(bf16[4,128,512]{2,1,0:T(8,128)(2,1)} %param.4) | copy-start | bytes 1572868
  29.3 92.2 %copy-start = (bf16[4,512,512]{1,2,0:T(8,128)(2,1)}, bf16[4,512,512]{1,2,0:T(8,128)(2,1)S(1)}, u32[]{:S(2)}) copy-start(bf16[4,512,512]{1,2,0:T(8,128)(2,1)S(1)} %convert_element_type.17) | copy-start | bytes 6291460
  121.5 56.6 %copy-start.2 = (s32[4]{0:T(128)S(1)}, s32[4]{0:T(128)}, u32[]{:S(2)}) copy-start(s32[4]{0:T(128)} %param.7) | copy-start | bytes 52
  170.6 26.7 %collective-permute-start = (f32[128,4,512]{2,0,1:T(8,128)}, f32[128,4,512]{2,0,1:T(8,128)S(1)}, u32[]{:S(2)}, u32[]{:S(2)}) collective-permute-start(f32[128,4,512]{2,0,1:T(8,128)} %reduce-scatter.2.cloned.1.call-done), channel_id=1, source_target_pairs={{0,128},{128,0},{4,132},{132,4},{8,136},{136,8},{12,140},{140,12},... | collective-permute-start | bytes 3145736 | tf_op jit(solution)/shard_map/ppermute | solution.py:14
  174.6 18.6 %all-to-all-start = ((f32[128,4,512]{0,1,2:T(4,128)}), f32[128,4,512]{0,1,2:T(4,128)S(1)}, u32[]{:S(2)}, u32[]{:S(2)}) async-start(f32[128,4,512]{0,1,2:T(4,128)} %copy.11), calls=%async_computation.1 | async-start | bytes 2097152 | tf_op jit(solution)/shard_map/all_to_all | solution.py:48
Sparse Core Ops, SparseCore 0:
  20.5 87.4 all-gather.1
  121.6 48.9 reduce-scatter.1
where the time goes:
time: 208 us; the launch traced here: 207 us
  waiting for transfers between devices  146 us (70%)
  local copies, waits for them, and re-layouts  14 us (7%)
  blocking collectives  13.8 us (7%)
  between operations  13.5 us (6%)
  matrix products  13.4 us (6%)
  starting transfers between devices  4.98 us (2%)
  other arithmetic  2.12 us (1%)
    all_gather x1, waiting for transfers between devices, body(): panels_all = lax.all_gather(blocks, 'pair', axis=1, tiled=True)  78.5 us
    reduce_scatter x1, waiting for transfers between devices, body(): lax.psum_scatter(jnp.einsum('qac,qpcb->apb', panel_cols, half_done, prefe...  49.1 us
    all_to_all x1, waiting for transfers between devices, body(): lax.all_to_all(own_rows, 'virt', split_axis=2, concat_axis=0, tiled=True)  15.1 us
    all_gather x1, blocking collectives, body(): blocks = lax.all_gather(panels, 'virt', axis=0, tiled=True)  13.8 us
    dot_general x1, matrix products, body(): jnp.einsum('qac,qpcb->apb', panel_cols, half_done, preferred_element_type...  13.4 us
    convert_element_type x2, local copies, waits for them, and re-layouts, body(): mask_full = expand_mask(domain, tile_size).astype(jnp.bfloat16)  5.53 us
  transfers between devices with their start and end apart: 4, of which 4 were waited for; matrix products, arithmetic and copies ran while one was open for 6% of the time, Pallas kernels for 0%

commit v1 on v0

v1 whole, which is shorter than its diff:
```python
import functools

import jax
import jax.numpy as jnp
from jax import lax
from jax.experimental import pallas as pl
from jax.experimental.pallas import tpu as pltpu
from jax.sharding import PartitionSpec as P

MESH = pl.DeviceIdType.MESH
NX, NY, NZ = 4, 4, 8
PAIRS_DEV, VW, TILE = 4, 512, 64
ROWS = VW // NX
TILES_B = ((1, 2), (1, 1))
TILES_C = ((3, 1), (2, 2))
F32, BF16 = jnp.float32, jnp.bfloat16


def dot_t(a, b):
    return lax.dot_general(a, b, (((1,), (1,)), ((), ())), preferred_element_type=F32)


class Slots:
    def __init__(self):
        self.names = {}

    def __getitem__(self, name):
        return self.names.setdefault(name, len(self.names))


def kernel(slots, amp_ref, pan_ref, dom_ref, mir_ref, out_ref,
           stg, xbuf, pst, bb, tacc, trecv, sout, land_low, land_up, send_sem, recv_sem, loc_sem):
    x = lax.axis_index("virt")
    p = lax.axis_index("pair")
    c = p % 2
    z = (p // 2) % NZ
    y = p // (2 * NZ)
    half = y // 2
    ybase = y % 2

    def dev(x_, y_, z_, c_):
        return ((y_ * NZ + z_) * 2 + c_, x_)

    def off(dx=0, dy=0, dz=0):
        return dev((x + dx) % NX, (y + dy) % NY, (z + dz) % NZ, c)

    sibling = dev(x, y, z, 1 - c)
    started = []

    def copy(src, dst, name, device):
        k = slots[name]
        return pltpu.make_async_remote_copy(
            src_ref=src, dst_ref=dst, send_sem=send_sem.at[k], recv_sem=recv_sem.at[k],
            device_id=device, device_id_type=MESH)

    def send(ref, name, device):
        cp = copy(ref, ref, name, device)
        cp.start()
        started.append(cp)

    def arrive(ref, name):
        copy(ref, ref, name, sibling).wait_recv()

    barrier = pltpu.get_barrier_semaphore()
    peers = [off(dz=d) for d in range(1, NZ)] + [off(dy=1), off(dy=3)]
    peers += [dev((x + dx) % NX, (y + dy) % NY, z, (c + dc) % 2)
              for dx in range(NX) for dy in (0, 2) for dc in range(2) if (dx, dy, dc) != (0, 0, 0)]
    for peer in peers:
        pl.semaphore_signal(barrier, inc=1, device_id=peer, device_id_type=MESH)
    pl.semaphore_wait(barrier, len(peers))

    k = slots["swap"]
    swap = pltpu.make_async_remote_copy(
        src_ref=pan_ref.at[1 - c], dst_ref=pst, send_sem=send_sem.at[k], recv_sem=recv_sem.at[k],
        device_id=sibling, device_id_type=MESH)
    swap.start()

    lane = lax.broadcasted_iota(jnp.int32, (1, 128), 1)
    order = []
    for i in range(PAIRS_DEV):
        found = jnp.int32(0)
        for q in range(PAIRS_DEV):
            found = jnp.where(mir_ref[q] % PAIRS_DEV == i, jnp.int32(q), found)
        order.append(jnp.where(half == 0, jnp.int32(i), found))
    for i in range(PAIRS_DEV):
        for h in range(2):
            row = 2 * x + h
            parts = [jnp.where(lane < TILE, dom_ref[order[i], row, 2 * t], dom_ref[order[i], row, 2 * t + 1])
                     for t in range(4)]
            mask = jnp.concatenate(parts, axis=1).astype(F32)
            rows = pl.ds(h * TILE, TILE)
            stg[i, rows, :] = (amp_ref[order[i], rows, :].astype(F32) * mask).astype(BF16)

    swap.wait()
    mine = pan_ref[c].astype(F32)
    other = pst[...].astype(F32)
    first = jnp.where(c == 0, mine, other)
    second = jnp.where(c == 0, other, mine)
    for j in range(2):
        rows16 = jnp.concatenate([first[8 * j:8 * j + 8], second[8 * j:8 * j + 8]], axis=0).astype(BF16)
        for t in range(4):
            bb[t, x, j, y, z] = rows16[:, 128 * t:128 * t + 128]

    def z1(z_):
        return bb.at[pl.ds(1, 3), x, :, y, z_]

    def x1(x_):
        return bb.at[0, x_, :, y, z]

    def y2(y_):
        return bb.at[0, :, :, y_, z]

    def ring_a(j, z_, part=None):
        return bb.at[0, slice(None) if part is None else pl.ds(2 * part, 2), j, :, z_]

    def line_b(j, x_):
        return bb.at[pl.ds(*TILES_B[j]), x_, j, y]

    def ring_b(j, y_, part=None):
        return bb.at[pl.ds(*TILES_B[j]), slice(None) if part is None else pl.ds(2 * part, 2), j, y_]

    def line_c(j, y_):
        return bb.at[pl.ds(*TILES_C[j]), x, j, y_]

    def ring_c(j, x_, part=None):
        return bb.at[pl.ds(*TILES_C[j]), x_, j, slice(None) if part is None else pl.ds(2 * part, 2)]

    for d in range(1, NX):
        send(x1(x), ("x1", d), off(dx=d))
    for d in (1, 7, 2, 6, 3, 5, 4):
        send(z1(z), ("z1", d), off(dz=d))

    def amp_slot(x_):
        return xbuf.at[half, pl.ds(pl.multiple_of(x_ * ROWS, ROWS), ROWS), :]

    for i in range(PAIRS_DEV):
        k = slots[("amp_s", i)]

        @pl.when(jnp.logical_not(jnp.logical_and(half == c, x == i)))
        def _():
            pltpu.make_async_remote_copy(
                src_ref=stg.at[i], dst_ref=amp_slot(x), send_sem=send_sem.at[k],
                recv_sem=recv_sem.at[slots[("amp", 0)] + x],
                device_id=dev(i, ybase + 2 * c, z, half), device_id_type=MESH).start()

        @pl.when(jnp.logical_and(half == c, x == i))
        def _():
            pltpu.make_async_copy(stg.at[i], amp_slot(x), loc_sem.at[0]).start()

    for d in range(1, NX):
        arrive(x1((x - d) % NX), ("x1", d))
    for d in range(1, NY):
        send(y2(y), ("y2", d), off(dy=d))
    for d in (1, 7, 2, 6, 3, 5, 4):
        arrive(z1((z - d) % NZ), ("z1", d))
    for j in range(2):
        for d in range(1, 4):
            send(line_b(j, x), ("lb", j, d), off(dx=d))
            send(line_c(j, y), ("lc", j, d), off(dy=d))

    for d in range(1, NY):
        arrive(y2((y - d) % NY), ("y2", d))

    def a_step(j, s):
        if s > 1:
            arrive(ring_a(j, (z - s + 1) % NZ), ("ra", j, 1, s - 1))
        send(ring_a(j, (z - s + 1) % NZ, 0 if s == 4 else None), ("ra", j, 1, s), off(dz=1))
        if s > 1:
            arrive(ring_a(j, (z + s - 1) % NZ), ("ra", j, 7, s - 1))
        send(ring_a(j, (z + s - 1) % NZ, 1 if s == 4 else None), ("ra", j, 7, s), off(dz=7))

    def b_step(j, s):
        if s == 1:
            for d in range(1, 4):
                arrive(line_b(j, (x - d) % NX), ("lb", j, d))
            for d in (1, 3):
                send(ring_b(j, y), ("rb", j, d, 1), off(dy=d))
        else:
            for d in (1, 3):
                arrive(ring_b(j, (y - d) % NY), ("rb", j, d, 1))
                send(ring_b(j, (y - d) % NY, d // 2), ("rb", j, d, 2), off(dy=d))

    def c_step(j, s):
        if s == 1:
            for d in range(1, 4):
                arrive(line_c(j, (y - d) % NY), ("lc", j, d))
            for d in (1, 3):
                send(ring_c(j, x), ("rc", j, d, 1), off(dx=d))
        else:
            for d in (1, 3):
                arrive(ring_c(j, (x - d) % NX), ("rc", j, d, 1))
                send(ring_c(j, (x - d) % NX, d // 2), ("rc", j, d, 2), off(dx=d))

    a_step(0, 1)
    a_step(1, 1)

    def amp_arrived(slot, x_):
        return xbuf.at[slot, pl.ds(x_ * ROWS, ROWS), :]

    for x_ in range(NX):
        here = amp_arrived(c, x_)

        @pl.when(jnp.logical_not(jnp.logical_and(half == c, x == x_)))
        def _():
            copy(here, here, ("amp", x_), sibling).wait_recv()

        @pl.when(jnp.logical_and(half == c, x == x_))
        def _():
            pltpu.make_async_copy(stg.at[0], here, loc_sem.at[0]).wait()

        send(here, ("fwd", x_), sibling)

    b_step(0, 1)
    c_step(0, 1)
    a_step(0, 2)
    a_step(1, 2)
    b_step(1, 1)
    c_step(1, 1)
    a_step(0, 3)
    a_step(1, 3)
    b_step(0, 2)
    c_step(0, 2)
    a_step(0, 4)
    a_step(1, 4)
    b_step(1, 2)
    c_step(1, 2)

    def last(j):
        arrive(ring_a(j, (z + 4) % NZ, 0), ("ra", j, 1, 4))
        arrive(ring_a(j, (z + 4) % NZ, 1), ("ra", j, 7, 4))
        for d in (1, 3):
            arrive(ring_b(j, (y + 2) % NY, d // 2), ("rb", j, d, 2))
            arrive(ring_c(j, (x + 2) % NX, d // 2), ("rc", j, d, 2))

    for x_ in range(NX):
        arrive(amp_arrived(1 - c, x_), ("fwd", x_))

    tacc[...] = jnp.zeros_like(tacc)
    for j in range(2):
        last(j)

        @pl.loop(0, NX)
        def _(x_):
            panel = jnp.concatenate([bb[t, x_, j].reshape(VW, 128) for t in range(4)], axis=1)
            done = dot_t(xbuf[0], panel).astype(BF16)
            tacc[...] += jnp.dot(panel, done, preferred_element_type=F32)
            turned = dot_t(panel, xbuf[1]).astype(BF16)
            tacc[...] += dot_t(turned, panel)

    k = slots["tswap"]
    tswap = pltpu.make_async_remote_copy(
        src_ref=tacc.at[pl.ds(pl.multiple_of((1 - c) * 256, 256), 256), :], dst_ref=trecv,
        send_sem=send_sem.at[k], recv_sem=recv_sem.at[k], device_id=sibling, device_id_type=MESH)
    tswap.start()
    tswap.wait()
    full = (tacc[pl.ds(pl.multiple_of(c * 256, 256), 256), :] + trecv[...]).astype(BF16)
    for t in range(4):
        sout[t] = full[:, 128 * t:128 * t + 128]

    def low_dst(i, c_):
        return land_low.at[i, pl.ds(pl.multiple_of(c_ * 256, 256), 256), :]

    for t in range(NX):
        k = slots[("low_s", t)]
        self_ = jnp.logical_and(jnp.logical_and(half == 0, c == 0), x == t)

        @pl.when(jnp.logical_not(self_))
        def _():
            pltpu.make_async_remote_copy(
                src_ref=sout.at[t], dst_ref=low_dst(x, c), send_sem=send_sem.at[k],
                recv_sem=recv_sem.at[slots[("low", 0)] + 2 * x + c],
                device_id=dev(t, ybase, z, half), device_id_type=MESH).start()

        @pl.when(self_)
        def _():
            pltpu.make_async_copy(sout.at[t], low_dst(x, c), loc_sem.at[1]).start()

    for h in range(2):
        k = slots[("up_s", h)]
        to = 2 * c + h
        self_ = jnp.logical_and(jnp.logical_and(half == 1, c == 1), x == to)

        @pl.when(jnp.logical_not(self_))
        def _():
            pltpu.make_async_remote_copy(
                src_ref=sout.at[:, pl.ds(128 * h, 128), :], dst_ref=land_up.at[x], send_sem=send_sem.at[k],
                recv_sem=recv_sem.at[slots[("up", 0)] + x],
                device_id=dev(to, ybase + 2, z, half), device_id_type=MESH).start()

        @pl.when(self_)
        def _():
            pltpu.make_async_copy(sout.at[:, pl.ds(128 * h, 128), :], land_up.at[x], loc_sem.at[1]).start()

    def mask_cols(i):
        return [jnp.where(lane < TILE, dom_ref[i, r, 2 * x], dom_ref[i, r, 2 * x + 1]).astype(F32) for r in range(8)]

    @pl.when(half == 0)
    def _():
        for i in range(PAIRS_DEV):
            for c_ in range(2):
                here = land_low.at[i, pl.ds(c_ * 256, 256), :]
                self_ = jnp.logical_and(jnp.logical_and(c == 0, x == i), c_ == 0)

                @pl.when(jnp.logical_not(self_))
                def _():
                    copy(here, here, ("low", i, c_), sibling).wait_recv()

                @pl.when(self_)
                def _():
                    pltpu.make_async_copy(sout.at[0], here, loc_sem.at[1]).wait()

            masks = mask_cols(i)
            for r in range(8):
                rows = pl.ds(r * TILE, TILE)
                out_ref[i, rows, :] = land_low[i, rows, :].astype(F32) * masks[r]

    @pl.when(half == 1)
    def _():
        for i in range(PAIRS_DEV):
            self_ = jnp.logical_and(c == 1, jnp.logical_and(x == i, x // 2 == 1))

            @pl.when(jnp.logical_not(self_))
            def _():
                copy(land_up.at[i], land_up.at[i], ("up", i), sibling).wait_recv()

            @pl.when(self_)
            def _():
                pltpu.make_async_copy(sout.at[:, pl.ds(0, 128), :], land_up.at[i], loc_sem.at[1]).wait()

        for i in range(PAIRS_DEV):
            masks = mask_cols(i)
            got = land_up[mir_ref[i] % PAIRS_DEV].astype(F32)
            for t in range(4):
                turned = got[t].T
                for h in range(2):
                    out_ref[i, pl.ds(128 * t + TILE * h, TILE), :] = turned[TILE * h:TILE * h + TILE] * masks[2 * t + h]

    for cp in started:
        cp.wait_send()
    for i in range(PAIRS_DEV):
        @pl.when(jnp.logical_not(jnp.logical_and(half == c, x == i)))
        def _():
            copy(stg.at[i], stg.at[i], ("amp_s", i), sibling).wait_send()
    for t in range(NX):
        @pl.when(jnp.logical_not(jnp.logical_and(jnp.logical_and(half == 0, c == 0), x == t)))
        def _():
            copy(sout.at[t], sout.at[t], ("low_s", t), sibling).wait_send()
    for h in range(2):
        @pl.when(jnp.logical_not(jnp.logical_and(jnp.logical_and(half == 1, c == 1), x == 2 * c + h)))
        def _():
            part = sout.at[:, pl.ds(128 * h, 128), :]
            copy(part, part, ("up_s", h), sibling).wait_send()


def body(amplitudes, panels, domain, mirror):
    slots = Slots()
    for i in range(NX):
        slots[("amp", i)]
    for i in range(NX):
        for c_ in range(2):
            slots[("low", i, c_)]
    slots.names[("low", 0)] = slots[("low", 0, 0)]
    for i in range(NX):
        slots[("up", i)]
    vm = pl.BlockSpec(memory_space=pltpu.VMEM)
    sm = pl.BlockSpec(memory_space=pltpu.SMEM)
    return pl.pallas_call(
        functools.partial(kernel, slots),
        out_shape=jax.ShapeDtypeStruct((PAIRS_DEV, VW, ROWS), F32),
        in_specs=[vm, vm, sm, sm],
        out_specs=vm,
        scratch_shapes=[
            pltpu.VMEM((PAIRS_DEV, ROWS, VW), BF16),
            pltpu.VMEM((2, VW, VW), BF16),
            pltpu.VMEM((16, VW), BF16),
            pltpu.VMEM((4, NX, 2, NY, NZ, 16, 128), BF16),
            pltpu.VMEM((VW, VW), F32),
            pltpu.VMEM((256, VW), F32),
            pltpu.VMEM((4, 256, 128), BF16),
            pltpu.VMEM((PAIRS_DEV, VW, ROWS), BF16),
            pltpu.VMEM((PAIRS_DEV, 4, 128, 128), BF16),
            pltpu.SemaphoreType.DMA((160,)),
            pltpu.SemaphoreType.DMA((160,)),
            pltpu.SemaphoreType.DMA((2,)),
        ],
        name="ladder",
        cost_estimate=pl.CostEstimate(flops=8 * 2**30, bytes_accessed=2 * 2**20, transcendentals=0),
        compiler_params=pltpu.CompilerParams(collective_id=0, has_side_effects=True, vmem_limit_bytes=48 * 2**20),
    )(amplitudes, panels.reshape(2, 16, VW), domain, mirror)


def solution(mesh):
    in_specs = (P("pair", "virt", None), P("virt", "pair", None), P("pair", None, None), P("pair"))
    out_specs = P("pair", None, "virt")
    return jax.shard_map(body, mesh=mesh, in_specs=in_specs, out_specs=out_specs, check_vma=False)
```

time: 208 us -> 67.7 us (0.33)
  waiting for transfers between devices: 146 us -> 0 us
  Pallas kernels: 0 us -> 63.3 us
  blocking collectives: 13.8 us -> 0 us
  between operations: 13.5 us -> 0.01 us
  matrix products: 13.4 us -> 0 us
  local copies, waits for them, and re-layouts: 14 us -> 4.14 us
  starting transfers between devices: 4.98 us -> 0 us
  other arithmetic: 2.12 us -> 0 us
    all_gather x1 -> x0, waiting for transfers between devices: 78.5 us -> none  [body(): panels_all = lax.all_gather(blocks, 'pair', axis=1, tiled=True)]
    pallas_call x0 -> x1, Pallas kernels: none -> 63.3 us  [body(): pl.pallas_call(functools.partial(kernel, slots), out_shape=jax.ShapeDtype...]
    reduce_scatter x1 -> x0, waiting for transfers between devices: 49.1 us -> none  [body(): lax.psum_scatter(jnp.einsum('qac,qpcb->apb', panel_cols, half_done, prefe...]
    all_to_all x1 -> x0, waiting for transfers between devices: 15.1 us -> none  [body(): lax.all_to_all(own_rows, 'virt', split_axis=2, concat_axis=0, tiled=True)]
    all_gather x1 -> x0, blocking collectives: 13.8 us -> none  [body(): blocks = lax.all_gather(panels, 'virt', axis=0, tiled=True)]
    dot_general x1 -> x0, matrix products: 13.4 us -> none  [body(): jnp.einsum('qac,qpcb->apb', panel_cols, half_done, preferred_element_type...]
    convert_element_type x2 -> x0, local copies, waits for them, and re-layouts: 5.53 us -> none  [body(): mask_full = expand_mask(domain, tile_size).astype(jnp.bfloat16)]
    unnamed x7 -> x9, local copies, waits for them, and re-layouts: 0.28 us -> 4.14 us
  transfers between devices with their start and end apart: 4 -> 0, of which waited for: 4 -> 0; matrix products, arithmetic and copies ran while one was open for 6% -> 0% of each run, Pallas kernels for 0% -> 0%
where the time goes in v1:
time: 67.7 us; the launch traced here: 67.4 us
  Pallas kernels  63.3 us (94%)
  local copies, waits for them, and re-layouts  4.14 us (6%)
    pallas_call x1, Pallas kernels, body(): pl.pallas_call(functools.partial(kernel, slots), out_shape=jax.ShapeDtype...  63.3 us
    unnamed x9, local copies, waits for them, and re-layouts  4.14 us

profile of v1, /device:TPU:24, one launch (start us, length us, event | category | flops | bytes accessed | tf_op | source)
XLA Modules:
  0.0 67.4 jit_solution(13666176423729893245)
XLA Ops:
  0.0 0.0 copy-start.3
  0.0 0.7 copy-done.3
  0.7 0.0 copy-start
  0.7 1.0 %copy-done = bf16[4,128,512]{2,1,0:T(8,128)(2,1)S(1)} copy-done((bf16[4,128,512]{2,1,0:T(8,128)(2,1)S(1)}, bf16[4,128,512]{2,1,0:T(8,128)(2,1)}, u32[]{:S(2)}) %copy-start) | copy-done | bytes 524312
  1.7 0.0 copy-start.1
  1.7 0.8 %copy-done.1 = bf16[4,8,512]{2,1,0:T(8,128)(2,1)S(1)} copy-done((bf16[4,8,512]{2,1,0:T(8,128)(2,1)S(1)}, bf16[4,8,512]{2,1,0:T(8,128)(2,1)}, u32[]{:S(2)}) %copy-start.1) | copy-done | bytes 32792
  2.5 0.0 copy-start.2
  2.5 0.7 %copy-done.2 = s32[4,8,8]{2,1,0:T(8,128)S(1)} copy-done((s32[4,8,8]{2,1,0:T(8,128)S(1)}, s32[4,8,8]{2,1,0:T(8,128)}, u32[]{:S(2)}) %copy-start.2) | copy-done | bytes 1048
  3.2 63.3 %ladder.1 = f32[4,512,128]{2,1,0:T(8,128)S(1)} custom-call(bf16[4,128,512]{2,1,0:T(8,128)(2,1)S(1)} %copy-done, bf16[2,16,512]{2,1,0:T(8,128)(2,1)S(1)} %bitcast.1, s32[4,8,8]{2,1,0:T(8,128)S(1)} %copy-done.2, s32[4]{0:T(128)S(1)} %copy-done.3), custom_call_target="tpu_custom_call" | custom-call | flops 8589934592 | bytes 2097152 | tf_op jit(solution)/shard_map/ladder/pallas_call | solution.py:367
  66.5 1.0 %copy.6 = f32[4,512,128]{2,1,0:T(8,128)} copy(f32[4,512,128]{2,1,0:T(8,128)S(1)} %ladder.1) | data formatting | bytes 2097152
Async XLA Ops:
  0.0 0.7 copy-start.3
  0.7 1.0 %copy-start = (bf16[4,128,512]{2,1,0:T(8,128)(2,1)S(1)}, bf16[4,128,512]{2,1,0:T(8,128)(2,1)}, u32[]{:S(2)}) copy-start(bf16[4,128,512]{2,1,0:T(8,128)(2,1)} %amp_ref.1) | copy-start | bytes 1572868
  1.7 0.8 %copy-start.1 = (bf16[4,8,512]{2,1,0:T(8,128)(2,1)S(1)}, bf16[4,8,512]{2,1,0:T(8,128)(2,1)}, u32[]{:S(2)}) copy-start(bf16[4,8,512]{2,1,0:T(8,128)(2,1)} %param.5) | copy-start | bytes 98308
  2.5 0.7 %copy-start.2 = (s32[4,8,8]{2,1,0:T(8,128)S(1)}, s32[4,8,8]{2,1,0:T(8,128)}, u32[]{:S(2)}) copy-start(s32[4,8,8]{2,1,0:T(8,128)} %dom_ref.1) | copy-start | bytes 3076

commit v2 on v0

v2 whole, which is shorter than its diff:
```python
import functools

import jax
import jax.numpy as jnp
from jax import lax
from jax.experimental import pallas as pl
from jax.experimental.pallas import tpu as pltpu
from jax.sharding import PartitionSpec as P

MESH = pl.DeviceIdType.MESH
NX, NY, NZ = 4, 4, 8
PAIRS_DEV, VW, TILE = 4, 512, 64
ROWS = VW // NX
PART_A = ((0, 1), (0, 2))
PART_B = (((1, 1, 0, 8), (2, 1, 0, 4)), ((2, 1, 0, 8),))
PART_C = (((3, 1, 0, 8), (2, 1, 4, 4)), ((3, 1, 0, 8),))
LINE = ((1, 3), (2, 2))
QUADS = (3, 2)
F32, BF16 = jnp.float32, jnp.bfloat16


def dot_t(a, b):
    return lax.dot_general(a, b, (((1,), (1,)), ((), ())), preferred_element_type=F32)


class Slots:
    def __init__(self):
        self.names = {}

    def __getitem__(self, name):
        return self.names.setdefault(name, len(self.names))


def kernel(slots, sends, amp_hbm, pan_hbm, dom_hbm, mir_hbm, out_ref,
           amp_ref, pan_ref, dom_ref, mir_ref, stg, xbuf, pst, bb, tacc, trecv, sout, land_low, land_up,
           send_sem, recv_sem, loc_sem):
    x = lax.axis_index("virt")
    p = lax.axis_index("pair")
    c = p % 2
    z = (p // 2) % NZ
    y = p // (2 * NZ)
    half = y // 2
    ybase = y % 2

    xs = [(x + d) % NX for d in range(NX)]
    ys = [(y + d) % NY for d in range(NY)]
    zs = [(z + d) % NZ for d in range(NZ)]

    def dev(x_, y_, z_, c_):
        return ((y_ * NZ + z_) * 2 + c_, x_)

    def off(dx=0, dy=0, dz=0):
        return dev(xs[dx], ys[dy], zs[dz], c)

    sibling = dev(x, y, z, 1 - c)

    def copy(src, dst, name, device, group):
        return pltpu.make_async_remote_copy(
            src_ref=src, dst_ref=dst, send_sem=send_sem.at[sends[group]], recv_sem=recv_sem.at[slots[name]],
            device_id=device, device_id_type=MESH)

    def send(src, dst, name, device, group):
        copy(src, dst, name, device, group).start()

    def arrive(ref, name):
        pltpu.make_async_copy(ref, ref, recv_sem.at[slots[name]]).wait()

    def all_sent(ref, group):
        pltpu.make_async_copy(ref, ref, send_sem.at[sends[group]]).wait()

    def size(t=1, j=1, r=1, y_=1, z_=1):
        return bb.at[pl.ds(0, t), pl.ds(0, j), pl.ds(0, r), pl.ds(0, y_), pl.ds(0, z_)]

    loads = [pltpu.make_async_copy(src, dst, loc_sem.at[i]) for i, (src, dst) in enumerate(
        ((dom_hbm, dom_ref), (mir_hbm, mir_ref), (pan_hbm, pan_ref), (amp_hbm, amp_ref)))]
    for load in loads:
        load.start()

    barrier = pltpu.get_barrier_semaphore()
    peers = [off(dz=d) for d in range(1, NZ)]
    peers += [off(dx=dx, dy=dy) for dx in range(NX) for dy in (1, 3)]
    peers += [dev(xs[dx], ys[dy], z, (c, 1 - c)[dc])
              for dx in range(NX) for dy in (0, 2) for dc in range(2) if (dx, dy, dc) != (0, 0, 0)]
    for peer in peers:
        pl.semaphore_signal(barrier, inc=1, device_id=peer, device_id_type=MESH)

    tacc[...] = jnp.zeros_like(tacc)
    for load in loads:
        load.wait()

    lane = lax.broadcasted_iota(jnp.int32, (1, 128), 1)
    order = []
    for i in range(PAIRS_DEV):
        found = jnp.int32(0)
        for q in range(PAIRS_DEV):
            found = jnp.where(mir_ref[q] % PAIRS_DEV == i, jnp.int32(q), found)
        order.append(jnp.where(half == 0, jnp.int32(i), found))
    for i in range(PAIRS_DEV):
        for h in range(2):
            row = 2 * x + h
            parts = [jnp.where(lane < TILE, dom_ref[order[i], row, 2 * t], dom_ref[order[i], row, 2 * t + 1])
                     for t in range(4)]
            mask = jnp.concatenate(parts, axis=1).astype(F32)
            rows = pl.ds(h * TILE, TILE)
            stg[i, rows, :] = (amp_ref[order[i], rows, :].astype(F32) * mask).astype(BF16)

    def amp_slot(x_):
        return xbuf.at[half, pl.ds(pl.multiple_of(x_ * ROWS, ROWS), ROWS), :]

    def move(here, src, dst, name, device, group):
        @pl.when(jnp.logical_not(here))
        def _():
            pltpu.make_async_remote_copy(
                src_ref=src, dst_ref=dst, send_sem=send_sem.at[sends[group]], recv_sem=recv_sem.at[name],
                device_id=device, device_id_type=MESH).start()

        @pl.when(here)
        def _():
            pltpu.make_async_copy(src, dst, recv_sem.at[name]).start()

    def send_amp(i):
        move(jnp.logical_and(half == c, x == i), stg.at[i], amp_slot(x), slots[("amp", 0)] + x,
             dev(i, ybase + 2 * c, z, half), "amp")

    pl.semaphore_wait(barrier, len(peers))

    swap = copy(pan_ref.at[1 - c], pst, "swap", sibling, "swap")
    swap.start()
    swap.wait()
    mine = pan_ref[c].astype(F32)
    other = pst[...].astype(F32)
    first = jnp.where(c == 0, mine, other)
    second = jnp.where(c == 0, other, mine)
    for j in range(2):
        rows16 = jnp.concatenate([first[8 * j:8 * j + 8], second[8 * j:8 * j + 8]], axis=0).astype(BF16)
        for t in range(4):
            bb[t, j, 0, y, z] = rows16[:, 128 * t:128 * t + 128]

    def plane_a(j, r, y_):
        return bb.at[pl.ds(*PART_A[j]), j, r, y_, z]

    def send_plane(j):
        for dy in (0, 1, 3, 2):
            for dx in (0, 1, 3, 2):
                if (dx, dy) != (0, 0):
                    send(plane_a(j, 0, y), plane_a(j, -dx % NX, y), ("pa", j), off(dx=dx, dy=dy), "pa")

    def arrive_plane(j):
        arrive(size(t=PART_A[j][1], y_=3, z_=5), ("pa", j))

    def line_z(j, z_):
        return bb.at[pl.ds(*LINE[j]), j, 0, y, z_]

    def send_z(j):
        for d in (1, 7, 2, 6, 3, 5, 4):
            send(line_z(j, z), line_z(j, z), ("z1", j), off(dz=d), ("z1", j))

    def arrive_z(j):
        arrive(size(t=LINE[j][1], z_=7), ("z1", j))

    def line(box, j, r, y_):
        return bb.at[pl.ds(box[0], box[1]), j, r, y_, pl.ds(box[2], box[3])]

    def send_lines(j):
        for d in (1, 3, 2):
            for box in PART_B[j]:
                send(line(box, j, 0, y), line(box, j, -d % NX, y), ("lb", j), off(dx=d), ("li", j))
            for box in PART_C[j]:
                send(line(box, j, 0, y), line(box, j, 0, y), ("lc", j), off(dy=d), ("li", j))

    def arrive_lines_b(j):
        arrive(size(y_=3, r=QUADS[j], z_=4), ("lb", j))

    def arrive_lines_c(j):
        arrive(size(y_=3, r=QUADS[j], z_=4), ("lc", j))

    def ring_a(n, z_, part=None):
        r = pl.ds(2 * (n % 2), 2) if part is None else pl.ds(2 * (n % 2) + part, 1)
        return bb.at[pl.ds(*PART_A[n // 2]), n // 2, r, :, z_]

    def step_a(n, s):
        for way, sign, part in ((1, -1, 0), (7, 1, 1)):
            here = zs[sign * (s - 1)]
            if s > 1:
                arrive(ring_a(n, here), ("ra", n, way, s - 1))
            ref = ring_a(n, here, part if s == 4 else None)
            send(ref, ref, ("ra", n, way, s), off(dz=way), "ra")

    def ring_b(n, box, y_, part=None):
        r = pl.ds(2 * (n % 2), 2) if part is None else pl.ds(2 * (n % 2) + part, 1)
        return bb.at[pl.ds(box[0], box[1]), n // 2, r, y_, pl.ds(box[2], box[3])]

    def step_b(n, s):
        for d in (1, 3):
            if s > 1:
                arrive(size(r=2, y_=QUADS[n // 2], z_=4), ("rb", n, d, 1))
            for box in PART_B[n // 2]:
                ref = ring_b(n, box, y) if s == 1 else ring_b(n, box, ys[-d], d // 2)
                send(ref, ref, ("rb", n, d, s), off(dy=d), "rb")

    def ring_c(j, box, r, part=None):
        some = slice(None) if part is None else pl.ds(2 * part, 2)
        return bb.at[pl.ds(box[0], box[1]), j, r, some, pl.ds(box[2], box[3])]

    def step_c(j, s):
        for d in (1, 3):
            if s > 1:
                arrive(size(r=4, y_=QUADS[j], z_=4), ("rc", j, d, 1))
            for box in PART_C[j]:
                if s == 1:
                    send(ring_c(j, box, 0), ring_c(j, box, 4 - d), ("rc", j, d, 1), off(dx=d), "rc")
                else:
                    send(ring_c(j, box, 4 - d, d // 2), ring_c(j, box, 2, d // 2), ("rc", j, d, 2), off(dx=d), "rc")

    def ready(n):
        for part, way in ((0, 1), (1, 7)):
            arrive(ring_a(n, zs[4], part), ("ra", n, way, 4))
        for d in (1, 3):
            arrive(size(y_=QUADS[n // 2], z_=4), ("rb", n, d, 2))
        if n % 2 == 1:
            for d in (1, 3):
                arrive(size(r=2, y_=QUADS[n // 2], z_=4), ("rc", n // 2, d, 2))

    def amp_arrived(slot, x_):
        return xbuf.at[slot, pl.ds(x_ * ROWS, ROWS), :]

    def forward_amp():
        for x_ in range(NX):
            here = amp_arrived(c, x_)
            arrive(here, ("amp", x_))
            send(here, here, "fwd", sibling, "fwd")

    send_plane(0)
    send_z(0)
    send_plane(1)
    send_z(1)
    for i in range(PAIRS_DEV):
        send_amp(i)
    arrive_plane(0)
    step_a(0, 1)
    step_a(1, 1)
    arrive_z(0)
    send_lines(0)
    arrive_plane(1)
    step_a(2, 1)
    step_a(3, 1)
    arrive_z(1)
    send_lines(1)
    step_a(0, 2)
    step_a(1, 2)
    step_a(2, 2)
    arrive_lines_b(0)
    step_b(0, 1)
    step_b(1, 1)
    arrive_lines_c(0)
    step_c(0, 1)
    step_a(3, 2)
    forward_amp()
    step_a(0, 3)
    step_a(1, 3)
    arrive_lines_b(1)
    step_b(2, 1)
    step_b(3, 1)
    arrive_lines_c(1)
    step_c(1, 1)
    step_a(2, 3)
    step_a(3, 3)
    step_b(0, 2)
    step_a(0, 4)
    step_b(1, 2)
    step_a(1, 4)
    step_c(0, 2)
    arrive(xbuf.at[1 - c], "fwd")

    def between(n, part):
        if (n, part) == (0, 0):
            step_b(2, 2)
            step_a(2, 4)
            step_b(3, 2)
            step_c(1, 2)
            step_a(3, 4)

    def panel(j, r):
        return jnp.concatenate([bb[t, j, r].reshape(VW, 128) for t in range(4)], axis=1)

    def panel_half(j, r, h):
        return jnp.concatenate([bb[t, j, r, pl.ds(2 * h, 2)].reshape(VW // 2, 128) for t in range(4)], axis=1)

    for n in range(3):
        ready(n)

        both = [panel(n >> 1, 2 * (n & 1) + r) for r in range(2)]
        wide = jnp.concatenate(both, axis=1)
        done = jnp.concatenate([dot_t(xbuf[0], b).astype(BF16) for b in both], axis=0)
        tacc[...] += jnp.dot(wide, done, preferred_element_type=F32)

        between(n, 0)
        both = [panel(n >> 1, 2 * (n & 1) + r) for r in range(2)]
        wide = jnp.concatenate(both, axis=1)
        turned = jnp.concatenate([dot_t(b, xbuf[1]).astype(BF16) for b in both], axis=1)
        tacc[...] += dot_t(turned, wide)
        between(n, 1)

    ready(3)
    both = [panel(1, 2 + r) for r in range(2)]
    wide = jnp.concatenate(both, axis=1)
    done = jnp.concatenate([dot_t(xbuf[0], b).astype(BF16) for b in both], axis=0)

    def half_rows(h):
        part = [panel_half(1, 2 + r, h) for r in range(2)]
        turned = jnp.concatenate([dot_t(b, xbuf[1]).astype(BF16) for b in part], axis=1)
        rows = pl.ds(pl.multiple_of(h * 256, 256), 256)
        return rows, tacc[rows, :] + jnp.dot(jnp.concatenate(part, axis=1), done, preferred_element_type=F32) + dot_t(
            turned, wide)

    rows, value = half_rows(1 - c)
    tacc[rows, :] = value
    tswap = copy(tacc.at[rows, :], trecv, "tswap", sibling, "tswap")
    tswap.start()
    rows, value = half_rows(c)
    tacc[rows, :] = value
    tswap.wait()
    full = (tacc[rows, :] + trecv[...]).astype(BF16)
    for t in range(4):
        sout[t] = full[:, 128 * t:128 * t + 128]

    low_self = jnp.logical_and(half == 0, c == 0)
    up_self = jnp.logical_and(jnp.logical_and(half == 1, c == 1), x >= 2)
    got = slots[("out", 0)] + x
    rows = pl.ds(pl.multiple_of(c * 256, 256), 256)
    for t in range(NX):
        move(jnp.logical_and(low_self, x == t), sout.at[t], land_low.at[x, rows, :], got, dev(t, ybase, z, half), "low")
    for h in range(2):
        to = 2 * c + h
        move(jnp.logical_and(up_self, x == to), sout.at[:, pl.ds(128 * h, 128), :], land_up.at[x], got,
             dev(to, ybase + 2, z, half), "up")

    def mask_cols(i):
        return [jnp.where(lane < TILE, dom_ref[i, r, 2 * x], dom_ref[i, r, 2 * x + 1]).astype(F32) for r in range(8)]

    all_sent(size(r=3, y_=3, z_=5), "pa")
    for j in range(2):
        all_sent(size(t=LINE[j][1], z_=7), ("z1", j))
        all_sent(size(j=2, r=3, y_=QUADS[j], z_=4), ("li", j))
    all_sent(size(t=3, r=4, y_=4, z_=7), "ra")
    all_sent(size(t=3, r=4, y_=4, z_=5), "rb")
    all_sent(size(t=3, r=4, y_=4, z_=5), "rc")
    all_sent(xbuf.at[c], "fwd")

    for i in range(PAIRS_DEV):
        arrive(land_up.at[i], ("out", i))

    @pl.when(half == 0)
    def _():
        for i in range(PAIRS_DEV):
            masks = mask_cols(i)
            for r in range(8):
                rows_ = pl.ds(r * TILE, TILE)
                out_ref[i, rows_, :] = (land_low[i, rows_, :].astype(F32) * masks[r]).astype(BF16)

    @pl.when(half == 1)
    def _():
        for i in range(PAIRS_DEV):
            masks = mask_cols(i)
            block = land_up[mir_ref[i] % PAIRS_DEV].astype(F32)
            for t in range(4):
                turned = block[t].T
                for h in range(2):
                    out_ref[i, pl.ds(128 * t + TILE * h, TILE), :] = (
                        turned[TILE * h:TILE * h + TILE] * masks[2 * t + h]).astype(BF16)

    def most_sent(short, whole, less, group):
        @pl.when(short)
        def _():
            all_sent(less, group)

        @pl.when(jnp.logical_not(short))
        def _():
            all_sent(whole, group)

    most_sent(half == c, stg, stg.at[pl.ds(0, 3)], "amp")
    most_sent(low_self, sout, sout.at[pl.ds(0, 3)], "low")
    most_sent(up_self, sout, sout.at[pl.ds(0, 2)], "up")


def body(amplitudes, panels, domain, mirror):
    slots, sends = Slots(), Slots()
    for i in range(NX):
        slots[("amp", i)]
    for i in range(NX):
        slots[("out", i)]
    vm = pl.BlockSpec(memory_space=pltpu.VMEM)
    hbm = pl.BlockSpec(memory_space=pltpu.HBM)
    return pl.pallas_call(
        functools.partial(kernel, slots, sends),
        out_shape=jax.ShapeDtypeStruct((PAIRS_DEV, VW, ROWS), BF16),
        in_specs=[hbm] * 4,
        out_specs=vm,
        scratch_shapes=[
            pltpu.VMEM((PAIRS_DEV, ROWS, VW), BF16),
            pltpu.VMEM((2, 16, VW), BF16),
            pltpu.SMEM((PAIRS_DEV, 8, 8), jnp.int32),
            pltpu.SMEM((PAIRS_DEV,), jnp.int32),
            pltpu.VMEM((PAIRS_DEV, ROWS, VW), BF16),
            pltpu.VMEM((2, VW, VW), BF16),
            pltpu.VMEM((16, VW), BF16),
            pltpu.VMEM((4, 2, NX, NY, NZ, 16, 128), BF16),
            pltpu.VMEM((VW, VW), F32),
            pltpu.VMEM((256, VW), F32),
            pltpu.VMEM((4, 256, 128), BF16),
            pltpu.VMEM((PAIRS_DEV, VW, ROWS), BF16),
            pltpu.VMEM((PAIRS_DEV, 4, 128, 128), BF16),
            pltpu.SemaphoreType.DMA((14,)),
            pltpu.SemaphoreType.DMA((75,)),
            pltpu.SemaphoreType.DMA((4,)),
        ],
        name="ladder",
        cost_estimate=pl.CostEstimate(flops=8 * 2**30, bytes_accessed=2 * 2**20, transcendentals=0),
        compiler_params=pltpu.CompilerParams(collective_id=0, has_side_effects=True, vmem_limit_bytes=56 * 2**20),
    )(amplitudes, panels.reshape(2, 16, VW), domain, mirror).astype(F32)


def solution(mesh):
    in_specs = (P("pair", "virt", None), P("virt", "pair", None), P("pair", None, None), P("pair"))
    out_specs = P("pair", None, "virt")
    return jax.shard_map(body, mesh=mesh, in_specs=in_specs, out_specs=out_specs, check_vma=False)
```

time: 208 us -> 57.8 us (0.28)
  waiting for transfers between devices: 146 us -> 0 us
  Pallas kernels: 0 us -> 55.6 us
  local copies, waits for them, and re-layouts: 14 us -> 0 us
  blocking collectives: 13.8 us -> 0 us
  between operations: 13.5 us -> 0.01 us
  matrix products: 13.4 us -> 0 us
  starting transfers between devices: 4.98 us -> 0 us
    all_gather x1 -> x0, waiting for transfers between devices: 78.5 us -> none  [body(): panels_all = lax.all_gather(blocks, 'pair', axis=1, tiled=True)]
    pallas_call x0 -> x1, Pallas kernels: none -> 55.6 us  [body(): pl.pallas_call(functools.partial(kernel, slots, sends), out_shape=jax.Sha...]
    reduce_scatter x1 -> x0, waiting for transfers between devices: 49.1 us -> none  [body(): lax.psum_scatter(jnp.einsum('qac,qpcb->apb', panel_cols, half_done, prefe...]
    all_to_all x1 -> x0, waiting for transfers between devices: 15.1 us -> none  [body(): lax.all_to_all(own_rows, 'virt', split_axis=2, concat_axis=0, tiled=True)]
    all_gather x1 -> x0, blocking collectives: 13.8 us -> none  [body(): blocks = lax.all_gather(panels, 'virt', axis=0, tiled=True)]
    dot_general x1 -> x0, matrix products: 13.4 us -> none  [body(): jnp.einsum('qac,qpcb->apb', panel_cols, half_done, preferred_element_type...]
    convert_element_type x2 -> x0, local copies, waits for them, and re-layouts: 5.53 us -> none  [body(): mask_full = expand_mask(domain, tile_size).astype(jnp.bfloat16)]
    all_to_all x1 -> x0, starting transfers between devices: 3.52 us -> none  [body(): lax.all_to_all(own_rows, 'virt', split_axis=2, concat_axis=0, tiled=True)]
  transfers between devices with their start and end apart: 4 -> 0, of which waited for: 4 -> 0; matrix products, arithmetic and copies ran while one was open for 6% -> 0% of each run, Pallas kernels for 0% -> 0%
where the time goes in v2:
time: 57.8 us; the launch traced here: 57.7 us
  Pallas kernels  55.6 us (96%)
  other arithmetic  2.08 us (4%)
    pallas_call x1, Pallas kernels, body(): pl.pallas_call(functools.partial(kernel, slots, sends), out_shape=jax.Sha...  55.6 us
    convert_element_type x1, other arithmetic, body(): return pl.pallas_call(functools.partial(kernel, slots, sends), out_shape=...  2.08 us

profile of v2, /device:TPU:24, one launch (start us, length us, event | category | flops | bytes accessed | tf_op | source)
XLA Modules:
  0.0 57.7 jit_solution(2333294460285661681)
XLA Ops:
  0.0 55.6 %ladder.1 = bf16[4,512,128]{2,1,0:T(8,128)(2,1)} custom-call(bf16[4,128,512]{2,1,0:T(8,128)(2,1)} %amp_hbm.1, bf16[2,16,512]{2,1,0:T(8,128)(2,1)} %bitcast.1, s32[4,8,8]{2,1,0:T(8,128)} %dom_hbm.1, s32[4]{0:T(128)} %mir_hbm.1), custom_call_target="tpu_custom_call" | custom-call | flops 8589934592 | bytes 2097152 | tf_op jit(solution)/shard_map/ladder/pallas_call | solution.py:394
  55.6 2.1 %convert_element_type.3 = f32[4,512,128]{2,1,0:T(8,128)} convert(bf16[4,512,128]{2,1,0:T(8,128)(2,1)} %ladder.1) | non-fusion elementwise | flops 262144 | bytes 1572864 | tf_op jit(solution)/shard_map/convert_element_type | solution.py:420

commit v3 on v2

--- a/solution.py
+++ b/solution.py
@@ -416,8 +416,8 @@
         ],
         name="ladder",
         cost_estimate=pl.CostEstimate(flops=8 * 2**30, bytes_accessed=2 * 2**20, transcendentals=0),
-        compiler_params=pltpu.CompilerParams(collective_id=0, has_side_effects=True, vmem_limit_bytes=56 * 2**20),
-    )(amplitudes, panels.reshape(2, 16, VW), domain, mirror).astype(F32)
+        compiler_params=pltpu.CompilerParams(collective_id=0, has_side_effects=True, vmem_limit_bytes=48 * 2**20),
+    )(*(pltpu.with_memory_space_constraint(a, pltpu.HBM) for a in (amplitudes, panels.reshape(2, 16, VW), domain, mirror))).astype(F32)
 
 
 def solution(mesh):

time: 57.8 us -> 56 us (0.969)
  other arithmetic: 2.08 us -> 1.04 us
  Pallas kernels: 55.6 us -> 54.8 us
    convert_element_type x1, other arithmetic: 2.08 us -> 1.04 us  [body(): return pl.pallas_call(functools.partial(kernel, slots, sends), out_shape=...]
    pallas_call x1, Pallas kernels: 55.6 us -> 54.8 us  [body(): pl.pallas_call(functools.partial(kernel, slots, sends), out_shape=jax.Sha...]
where the time goes in v3:
time: 56 us; the launch traced here: 55.8 us
  Pallas kernels  54.8 us (98%)
  other arithmetic  1.04 us (2%)
    pallas_call x1, Pallas kernels, body(): pl.pallas_call(functools.partial(kernel, slots, sends), out_shape=jax.Sha...  54.8 us

profile of v3, /device:TPU:24, one launch (start us, length us, event | category | flops | bytes accessed | tf_op | source)
XLA Modules:
  0.0 55.8 jit_solution(9877909238740857836)
XLA Ops:
  0.0 54.8 %ladder.1 = bf16[4,512,128]{2,1,0:T(8,128)(2,1)S(1)} custom-call(bf16[4,128,512]{2,1,0:T(8,128)(2,1)} %amp_hbm.1, bf16[2,16,512]{2,1,0:T(8,128)(2,1)} %bitcast.1, s32[4,8,8]{2,1,0:T(8,128)} %dom_hbm.1, s32[4]{0:T(128)} %mir_hbm.1), custom_call_target="tpu_custom_call" | custom-call | flops 8589934592 | bytes 2097152 | tf_op jit(solution)/shard_map/ladder/pallas_call | solution.py:394
  54.8 1.0 %convert_element_type.3 = f32[4,512,128]{2,1,0:T(8,128)} convert(bf16[4,512,128]{2,1,0:T(8,128)(2,1)S(1)} %ladder.1) | non-fusion elementwise | flops 262144 | bytes 1572864 | tf_op jit(solution)/shard_map/convert_element_type | solution.py:420

commit v4 on v3

--- a/solution.py
+++ b/solution.py
@@ -32,7 +32,7 @@
 
 
 def kernel(slots, sends, amp_hbm, pan_hbm, dom_hbm, mir_hbm, out_ref,
-           amp_ref, pan_ref, dom_ref, mir_ref, stg, xbuf, pst, bb, tacc, trecv, sout, land_low, land_up,
+           amp_ref, pan_ref, dom_ref, mir_ref, stg, xbuf, pst, bb, tacc, trecv, dn, sout, land_low, land_up,
            send_sem, recv_sem, loc_sem):
     x = lax.axis_index("virt")
     p = lax.axis_index("pair")
@@ -118,8 +118,9 @@
         def _():
             pltpu.make_async_copy(src, dst, recv_sem.at[name]).start()
 
-    def send_amp(i):
-        move(jnp.logical_and(half == c, x == i), stg.at[i], amp_slot(x), slots[("amp", 0)] + x,
+    def send_amp(d):
+        i = xs[d]
+        move(jnp.logical_and(half == c, d == 0), stg.at[i], amp_slot(x), slots[("amp", 0)] + x,
              dev(i, ybase + 2 * c, z, half), "amp")
 
     pl.semaphore_wait(barrier, len(peers))
@@ -234,8 +235,8 @@
     send_z(0)
     send_plane(1)
     send_z(1)
-    for i in range(PAIRS_DEV):
-        send_amp(i)
+    for d in (1, 3, 2, 0):
+        send_amp(d)
     arrive_plane(0)
     step_a(0, 1)
     step_a(1, 1)
@@ -286,39 +287,38 @@
     def panel_half(j, r, h):
         return jnp.concatenate([bb[t, j, r, pl.ds(2 * h, 2)].reshape(VW // 2, 128) for t in range(4)], axis=1)
 
-    for n in range(3):
+    def first_sum(n):
+        both = [panel(n >> 1, 2 * (n & 1) + r) for r in range(2)]
+        done = jnp.concatenate([dot_t(xbuf[0], b).astype(BF16) for b in both], axis=0)
+        tacc[...] += jnp.dot(jnp.concatenate(both, axis=1), done, preferred_element_type=F32)
+
+    for n in range(2):
         ready(n)
-
-        both = [panel(n >> 1, 2 * (n & 1) + r) for r in range(2)]
-        wide = jnp.concatenate(both, axis=1)
-        done = jnp.concatenate([dot_t(xbuf[0], b).astype(BF16) for b in both], axis=0)
-        tacc[...] += jnp.dot(wide, done, preferred_element_type=F32)
-
+        first_sum(n)
         between(n, 0)
         both = [panel(n >> 1, 2 * (n & 1) + r) for r in range(2)]
-        wide = jnp.concatenate(both, axis=1)
         turned = jnp.concatenate([dot_t(b, xbuf[1]).astype(BF16) for b in both], axis=1)
-        tacc[...] += dot_t(turned, wide)
+        tacc[...] += dot_t(turned, jnp.concatenate(both, axis=1))
         between(n, 1)
 
-    ready(3)
-    both = [panel(1, 2 + r) for r in range(2)]
-    wide = jnp.concatenate(both, axis=1)
-    done = jnp.concatenate([dot_t(xbuf[0], b).astype(BF16) for b in both], axis=0)
+    for n in (2, 3):
+        ready(n)
+        for r in range(2):
+            dn[2 * (n - 2) + r] = dot_t(xbuf[0], panel(1, 2 * (n - 2) + r)).astype(BF16)
 
     def half_rows(h):
-        part = [panel_half(1, 2 + r, h) for r in range(2)]
+        rows = pl.ds(pl.multiple_of(h * 256, 256), 256)
+        part = [panel_half(1, r, h) for r in range(NX)]
         turned = jnp.concatenate([dot_t(b, xbuf[1]).astype(BF16) for b in part], axis=1)
-        rows = pl.ds(pl.multiple_of(h * 256, 256), 256)
-        return rows, tacc[rows, :] + jnp.dot(jnp.concatenate(part, axis=1), done, preferred_element_type=F32) + dot_t(
-            turned, wide)
-
-    rows, value = half_rows(1 - c)
-    tacc[rows, :] = value
+        tacc[rows, :] += jnp.dot(
+            jnp.concatenate(part, axis=1), dn[...].reshape(NX * VW, VW), preferred_element_type=F32
+        ) + dot_t(turned, jnp.concatenate([panel(1, r) for r in range(NX)], axis=1))
+        return rows
+
+    rows = half_rows(1 - c)
     tswap = copy(tacc.at[rows, :], trecv, "tswap", sibling, "tswap")
     tswap.start()
-    rows, value = half_rows(c)
-    tacc[rows, :] = value
+    rows = half_rows(c)
     tswap.wait()
     full = (tacc[rows, :] + trecv[...]).astype(BF16)
     for t in range(4):
@@ -328,8 +328,9 @@
     up_self = jnp.logical_and(jnp.logical_and(half == 1, c == 1), x >= 2)
     got = slots[("out", 0)] + x
     rows = pl.ds(pl.multiple_of(c * 256, 256), 256)
-    for t in range(NX):
-        move(jnp.logical_and(low_self, x == t), sout.at[t], land_low.at[x, rows, :], got, dev(t, ybase, z, half), "low")
+    for d in (1, 3, 2, 0):
+        t = xs[d]
+        move(jnp.logical_and(low_self, d == 0), sout.at[t], land_low.at[x, rows, :], got, dev(t, ybase, z, half), "low")
     for h in range(2):
         to = 2 * c + h
         move(jnp.logical_and(up_self, x == to), sout.at[:, pl.ds(128 * h, 128), :], land_up.at[x], got,
@@ -407,6 +408,7 @@
             pltpu.VMEM((4, 2, NX, NY, NZ, 16, 128), BF16),
             pltpu.VMEM((VW, VW), F32),
             pltpu.VMEM((256, VW), F32),
+            pltpu.VMEM((NX, VW, VW), BF16),
             pltpu.VMEM((4, 256, 128), BF16),
             pltpu.VMEM((PAIRS_DEV, VW, ROWS), BF16),
             pltpu.VMEM((PAIRS_DEV, 4, 128, 128), BF16),

time: 56 us -> 55.3 us (0.987)
  Pallas kernels: 54.8 us -> 53.7 us
    pallas_call x1, Pallas kernels: 54.8 us -> 53.7 us  [body(): pl.pallas_call(functools.partial(kernel, slots, sends), out_shape=jax.Sha...]
where the time goes in v4:
time: 55.3 us; the launch traced here: 54.8 us
  Pallas kernels  53.7 us (97%)
  other arithmetic  1.04 us (2%)
    pallas_call x1, Pallas kernels, body(): pl.pallas_call(functools.partial(kernel, slots, sends), out_shape=jax.Sha...  53.7 us

profile of v4, /device:TPU:24, one launch (start us, length us, event | category | flops | bytes accessed | tf_op | source)
XLA Modules:
  0.0 54.8 jit_solution(15442335961135623431)
XLA Ops:
  0.0 53.7 %ladder.1 = bf16[4,512,128]{2,1,0:T(8,128)(2,1)S(1)} custom-call(bf16[4,128,512]{2,1,0:T(8,128)(2,1)} %amp_hbm.1, bf16[2,16,512]{2,1,0:T(8,128)(2,1)} %bitcast.1, s32[4,8,8]{2,1,0:T(8,128)} %dom_hbm.1, s32[4]{0:T(128)} %mir_hbm.1), custom_call_target="tpu_custom_call" | custom-call | flops 8589934592 | bytes 2097152 | tf_op jit(solution)/shard_map/ladder/pallas_call | solution.py:395
  53.7 1.0 %convert_element_type.3 = f32[4,512,128]{2,1,0:T(8,128)} convert(bf16[4,512,128]{2,1,0:T(8,128)(2,1)S(1)} %ladder.1) | non-fusion elementwise | flops 262144 | bytes 1572864 | tf_op jit(solution)/shard_map/convert_element_type | solution.py:422

commit v5 on v4

--- a/solution.py
+++ b/solution.py
@@ -11,11 +11,11 @@
 NX, NY, NZ = 4, 4, 8
 PAIRS_DEV, VW, TILE = 4, 512, 64
 ROWS = VW // NX
-PART_A = ((0, 1), (0, 2))
-PART_B = (((1, 1, 0, 8), (2, 1, 0, 4)), ((2, 1, 0, 8),))
-PART_C = (((3, 1, 0, 8), (2, 1, 4, 4)), ((3, 1, 0, 8),))
-LINE = ((1, 3), (2, 2))
-QUADS = (3, 2)
+PART_A = ((0, 2), (0, 1))
+PART_B = (((2, 1, 0, 8),), ((1, 1, 0, 8), (2, 1, 0, 4)))
+PART_C = (((3, 1, 0, 8),), ((3, 1, 0, 8), (2, 1, 4, 4)))
+LINE = ((2, 2), (1, 3))
+QUADS = (2, 3)
 F32, BF16 = jnp.float32, jnp.bfloat16
 
 

time: 55.3 us -> 54.3 us (0.982)
  Pallas kernels: 53.7 us -> 52.7 us
    pallas_call x1, Pallas kernels: 53.7 us -> 52.7 us  [body(): pl.pallas_call(functools.partial(kernel, slots, sends), out_shape=jax.Sha...]
where the time goes in v5:
time: 54.3 us; the launch traced here: 53.8 us
  Pallas kernels  52.7 us (97%)
  other arithmetic  1.04 us (2%)
    pallas_call x1, Pallas kernels, body(): pl.pallas_call(functools.partial(kernel, slots, sends), out_shape=jax.Sha...  52.7 us

profile of v5, /device:TPU:24, one launch (start us, length us, event | category | flops | bytes accessed | tf_op | source)
XLA Modules:
  0.0 53.8 jit_solution(13089485969454915059)
XLA Ops:
  0.0 52.7 %ladder.1 = bf16[4,512,128]{2,1,0:T(8,128)(2,1)S(1)} custom-call(bf16[4,128,512]{2,1,0:T(8,128)(2,1)} %amp_hbm.1, bf16[2,16,512]{2,1,0:T(8,128)(2,1)} %bitcast.1, s32[4,8,8]{2,1,0:T(8,128)} %dom_hbm.1, s32[4]{0:T(128)} %mir_hbm.1), custom_call_target="tpu_custom_call" | custom-call | flops 8589934592 | bytes 2097152 | tf_op jit(solution)/shard_map/ladder/pallas_call | solution.py:395
  52.8 1.0 %convert_element_type.3 = f32[4,512,128]{2,1,0:T(8,128)} convert(bf16[4,512,128]{2,1,0:T(8,128)(2,1)S(1)} %ladder.1) | non-fusion elementwise | flops 262144 | bytes 1572864 | tf_op jit(solution)/shard_map/convert_element_type | solution.py:422

commit v6 on v5

--- a/solution.py
+++ b/solution.py
@@ -153,7 +153,7 @@
         return bb.at[pl.ds(*LINE[j]), j, 0, y, z_]
 
     def send_z(j):
-        for d in (1, 7, 2, 6, 3, 5, 4):
+        for d in (4, 3, 5, 2, 6, 1, 7):
             send(line_z(j, z), line_z(j, z), ("z1", j), off(dz=d), ("z1", j))
 
     def arrive_z(j):
@@ -163,7 +163,7 @@
         return bb.at[pl.ds(box[0], box[1]), j, r, y_, pl.ds(box[2], box[3])]
 
     def send_lines(j):
-        for d in (1, 3, 2):
+        for d in (2, 1, 3):
             for box in PART_B[j]:
                 send(line(box, j, 0, y), line(box, j, -d % NX, y), ("lb", j), off(dx=d), ("li", j))
             for box in PART_C[j]:
@@ -235,7 +235,7 @@
     send_z(0)
     send_plane(1)
     send_z(1)
-    for d in (1, 3, 2, 0):
+    for d in (2, 1, 3, 0):
         send_amp(d)
     arrive_plane(0)
     step_a(0, 1)
@@ -328,7 +328,7 @@
     up_self = jnp.logical_and(jnp.logical_and(half == 1, c == 1), x >= 2)
     got = slots[("out", 0)] + x
     rows = pl.ds(pl.multiple_of(c * 256, 256), 256)
-    for d in (1, 3, 2, 0):
+    for d in (2, 1, 3, 0):
         t = xs[d]
         move(jnp.logical_and(low_self, d == 0), sout.at[t], land_low.at[x, rows, :], got, dev(t, ybase, z, half), "low")
     for h in range(2):

time: 54.3 us -> 54.4 us (level)
  no operation moved by 1% of the time
where the time goes in v6:
time: 54.4 us; the launch traced here: 54.1 us
  Pallas kernels  53.1 us (98%)
  other arithmetic  1.04 us (2%)
    pallas_call x1, Pallas kernels, body(): pl.pallas_call(functools.partial(kernel, slots, sends), out_shape=jax.Sha...  53.1 us

profile of v6, /device:TPU:24, one launch (start us, length us, event | category | flops | bytes accessed | tf_op | source)
XLA Modules:
  0.0 54.1 jit_solution(1367589205802460008)
XLA Ops:
  0.0 53.1 %ladder.1 = bf16[4,512,128]{2,1,0:T(8,128)(2,1)S(1)} custom-call(bf16[4,128,512]{2,1,0:T(8,128)(2,1)} %amp_hbm.1, bf16[2,16,512]{2,1,0:T(8,128)(2,1)} %bitcast.1, s32[4,8,8]{2,1,0:T(8,128)} %dom_hbm.1, s32[4]{0:T(128)} %mir_hbm.1), custom_call_target="tpu_custom_call" | custom-call | flops 8589934592 | bytes 2097152 | tf_op jit(solution)/shard_map/ladder/pallas_call | solution.py:395
  53.1 1.0 %convert_element_type.3 = f32[4,512,128]{2,1,0:T(8,128)} convert(bf16[4,512,128]{2,1,0:T(8,128)(2,1)S(1)} %ladder.1) | non-fusion elementwise | flops 262144 | bytes 1572864 | tf_op jit(solution)/shard_map/convert_element_type | solution.py:422
